TPU v7x, 512 devices: a whole 4x8x8 slice. The times are simulated.
512 devices in a mesh: tower: 16 (over x, y_hi), rank: 32 (over y_lo, z, core).
Axes of the slice: x: 4, y: 8 (y_hi: 4, y_lo: 2; y = y_hi * 2 + y_lo), z: 8, core: 2. Of those that a mesh axis runs over, the one named last changes fastest.
Arguments:
- pooled: bfloat16 [2, 8192, 16384], P(None, ('tower', 'rank')), may hold values from -8 to 8
- feature_order: int32 [16, 4], P('tower'), may hold values from 0 to 3, as said below
- cross_weight: bfloat16 [16, 3, 512, 512], P('tower'), may hold values from -0.25 to 0.25
- cross_bias: float32 [16, 3, 512], P('tower'), may hold values from -3 to 3
- compress_weight: bfloat16 [16, 128, 512], P('tower'), may hold values from -0.25 to 0.25
- norm_gain: float32 [16, 128], P('tower'), may hold values from 0.1 to 1.9
- mlp_weight: bfloat16 [4096, 2048], P(('tower', 'rank')), may hold values from -0.125 to 0.125
- mlp_bias: bfloat16 [4096], P(('tower', 'rank')), may hold values from -3 to 3
- out_weight: bfloat16 [4096], P(('tower', 'rank')), may hold values from -0.09375 to 0.09375
Outputs:
- logits: float32 [2, 32, 512], P(None, 'rank', 'tower')
Inputs may be any that keep to these rules, and one draw needn't show every extreme that they name: `feature_order`: each row is an ordering of 0 to 3.
All inputs are finite; a program needn't handle non-finite values.
Results may differ from a plain program's by a relative error of at most 0.0076.
Values may be sent and summed in bfloat16 or wider, within the bound.
No kernel may reach another device: no remote copies, remote signals or barrier semaphores. Data moves between devices by JAX's collectives and lax.ppermute only.
A program may use at most 64 MiB of HBM per device.

v0:
```python
import math
import jax
import jax.numpy as jnp
from jax import lax
from jax.sharding import PartitionSpec as P

E = 128
CD = 128
epsilon = 1e-06


def side_by_side(arrays, axis, dim, along):
    widths = [math.prod(a.shape[along:]) for a in arrays]
    both = jnp.concatenate(
        [a.reshape(*a.shape[:along], w) for a, w in zip(arrays, widths)], axis=along
    )
    whole = lax.all_gather(both, axis, axis=dim, tiled=True)
    parts = jnp.split(whole, [sum(widths[:k]) for k in range(1, len(widths))], axis=along)
    return tuple((b.reshape(*whole.shape[:along], *a.shape[along:]) for a, b in zip(arrays, parts)))


def in_blocks(x, dim, devices):
    shape = x.shape
    parts = x.reshape(*shape[:dim], devices, shape[dim] // devices, *shape[dim + 1 :])
    return jnp.moveaxis(parts, dim, 0)


def summed_on_arrival(x, axis, dim):
    parts = in_blocks(x, dim, lax.axis_size(axis))
    arrived = lax.all_to_all(parts, axis, split_axis=0, concat_axis=0, tiled=True)
    return arrived.sum(axis=0)


def tower_block(first, weights, biases, compress, gain):
    first_f = first.astype(jnp.float32)
    current = first
    for layer in range(weights.shape[0]):
        product = (
            jnp.dot(weights[layer], current, preferred_element_type=jnp.float32)
            + biases[layer][:, None]
        )
        current = (first_f * product + current.astype(jnp.float32)).astype(jnp.bfloat16)
    squeezed = jnp.dot(compress, current, preferred_element_type=jnp.float32)
    inverse_rms = lax.rsqrt(jnp.mean(squeezed * squeezed, axis=0, keepdims=True) + epsilon)
    return (squeezed * inverse_rms * gain[:, None]).astype(jnp.bfloat16)


def interact(joined):
    samples_now = joined.shape[1]
    values_f = joined.astype(jnp.float32).reshape(-1, CD, samples_now)
    gram = jnp.einsum("tck,uck->tuk", values_f, values_f, precision=lax.Precision.HIGHEST) / CD
    mixed = values_f + jnp.einsum("tuk,uck->tck", gram, values_f, precision=lax.Precision.HIGHEST)
    return mixed.reshape(-1, samples_now).astype(jnp.bfloat16)


def logit_terms(hidden_rows, hidden_bias, hidden_out, features):
    hidden = (
        jnp.dot(hidden_rows, features, preferred_element_type=jnp.float32)
        + hidden_bias.astype(jnp.float32)[:, None]
    )
    return jnp.sum(
        jax.nn.relu(hidden) * hidden_out.astype(jnp.float32)[:, None], axis=0, keepdims=True
    )


def on_device(
    pooled,
    feature_order,
    cross_weight,
    cross_bias,
    compress_weight,
    norm_gain,
    mlp_weight,
    mlp_bias,
    out_weight,
):
    micro_count = pooled.shape[0]
    arriving = [
        lax.all_to_all(pooled[batch], "rank", split_axis=1, concat_axis=0, tiled=True)
        for batch in range(micro_count)
    ]
    hidden_rows, hidden_bias, hidden_out = side_by_side(
        (mlp_weight, mlp_bias, out_weight), "tower", 0, 1
    )
    results = []
    for batch in range(micro_count):
        arrived = arriving[batch]
        samples_here = arrived.shape[1]
        first = jnp.take(arrived.reshape(-1, E, samples_here), feature_order[0], axis=0).reshape(
            -1, samples_here
        )
        compressed = tower_block(
            first, cross_weight[0], cross_bias[0], compress_weight[0], norm_gain[0]
        )
        tower_parts = lax.all_to_all(compressed, "tower", split_axis=1, concat_axis=0, tiled=True)
        mixed = interact(tower_parts)
        partial_value = logit_terms(
            hidden_rows, hidden_bias, hidden_out, lax.all_gather(mixed, "rank", axis=1, tiled=True)
        )
        logit_row = summed_on_arrival(partial_value, "rank", 1)
        results.append(logit_row)
    return jnp.stack(results)


def solution(mesh):
    return jax.shard_map(
        on_device,
        mesh=mesh,
        in_specs=(
            P(None, ("tower", "rank"), None),
            P("tower", None),
            P("tower", None, None, None),
            P("tower", None, None),
            P("tower", None, None),
            P("tower", None),
            P(("tower", "rank"), None),
            P(("tower", "rank")),
            P(("tower", "rank")),
        ),
        out_specs=P(None, "rank", "tower"),
        check_vma=False,
    )
```

profile of v0, /device:TPU:1, one launch (start us, length us, event | category | flops | bytes accessed | tf_op | source)
XLA Modules:
  0.0 249.7 jit_solution(15419998319595481402)
XLA Ops:
  6.5 1.3 fusion.58
  8.0 1.1 copy.64
  9.1 13.0 %all-to-all-start = ((bf16[16,32,512]{2,0,1:T(8,128)(2,1)}), bf16[16,32,512]{2,0,1:T(8,128)(2,1)S(1)}, u32[]{:S(2)}, u32[]{:S(2)}) async-start(bf16[16,32,512]{2,0,1:T(8,128)(2,1)} %copy.64), calls=%async_computation | async-start | bytes 1048576 | tf_op jit(solution)/shard_map/all_to_all | solution.py:79
  22.3 1.1 copy.72
  23.4 14.4 %all-to-all-done = bf16[16,32,512]{2,0,1:T(8,128)(2,1)S(1)} async-done(((bf16[16,32,512]{2,0,1:T(8,128)(2,1)}), bf16[16,32,512]{2,0,1:T(8,128)(2,1)S(1)}, u32[]{:S(2)}, u32[]{:S(2)}) %all-to-all-start) | async-done | bytes 524320 | tf_op jit(solution)/shard_map/all_to_all | solution.py:79
  37.8 5.5 %all-to-all-start.3 = ((bf16[16,32,512]{2,0,1:T(8,128)(2,1)}), bf16[16,32,512]{2,0,1:T(8,128)(2,1)S(1)}, u32[]{:S(2)}, u32[]{:S(2)}) async-start(bf16[16,32,512]{2,0,1:T(8,128)(2,1)} %copy.72), calls=%async_computation.3 | async-start | bytes 1048576 | tf_op jit(solution)/shard_map/all_to_all | solution.py:79
  43.4 0.6 gather_fusion
  44.0 15.0 %all-to-all-done.3 = bf16[16,32,512]{2,0,1:T(8,128)(2,1)S(1)} async-done(((bf16[16,32,512]{2,0,1:T(8,128)(2,1)}), bf16[16,32,512]{2,0,1:T(8,128)(2,1)S(1)}, u32[]{:S(2)}, u32[]{:S(2)}) %all-to-all-start.3) | async-done | bytes 524320 | tf_op jit(solution)/shard_map/all_to_all | solution.py:79
  59.0 0.6 gather_fusion.1
  60.2 1.7 fusion.11
  61.9 0.5 fusion.10
  62.4 1.3 fusion.14
  63.7 0.5 fusion.12
  64.3 0.9 copy-done.7
  65.1 2.0 multiply_reduce_fusion
  67.2 0.8 multiply_reduce_fusion.1
  68.3 18.7 %all_to_all.68 = bf16[128,16,32]{0,2,1:T(8,128)(2,1)S(1)} all-to-all(bf16[128,16,32]{0,2,1:T(8,128)(2,1)S(1)} %bitcast.175), channel_id=1, replica_groups=mesh['tower'=16,'rank'=32] {'tower'}, dimensions={1} | all-to-all | bytes 262144 | tf_op jit(solution)/shard_map/all_to_all | solution.py:95
  87.6 0.7 copy.99
  88.3 12.3 %all_to_all.69 = bf16[128,16,32]{0,2,1:T(8,128)(2,1)S(1)} all-to-all(bf16[128,16,32]{0,2,1:T(8,128)(2,1)S(1)} %bitcast.174), channel_id=1, replica_groups=mesh['tower'=16,'rank'=32] {'tower'}, dimensions={1} | all-to-all | bytes 262144 | tf_op jit(solution)/shard_map/all_to_all | solution.py:95
  100.9 0.4 fusion.29
  101.3 0.7 copy.98
  102.3 38.0 %all_gather.9 = bf16[128,2050]{1,0:T(8,128)(2,1)S(1)} all-gather(bf16[8,2050]{1,0:T(8,128)(2,1)S(1)} %concatenate.3), channel_id=1, replica_groups=mesh['tower'=16,'rank'=32] {'tower'}, dimensions={0}, use_global_device_ids=true | all-gather | bytes 557600 | tf_op jit(solution)/shard_map/all_gather | solution.py:17
  140.4 11.5 %all-gather.3.cloned.1.call-done = bf16[2048,1024]{0,1:T(8,128)(2,1)} async-done(((bf16[2048,32]{0,1:T(8,128)(2,1)}), bf16[2048,1024]{0,1:T(8,128)(2,1)}) %all-gather.3.cloned.1.call-update) | async-done | bytes 4194320 | tf_op jit(solution)/shard_map/all_gather | solution.py:98
  152.0 3.7 %fusion.23 = f32[1024]{0:T(1024)S(1)} fusion(bf16[2048,1024]{0,1:T(8,128)(2,1)} %all-gather.3.cloned.1.call-done, bf16[128,2050]{1,0:T(8,128)(2,1)S(1)} %all_gather.9, f32[128]{0:T(128)S(1)} %get-tuple-element.7, f32[128]{0:T(128)S(1)} %get-tuple-element.6), kind=kOutput, calls=%fused_computation.41 | convolution fusion | flops 537394176 | bytes 4723712 | tf_op jit(solution)/shard_map/dot_general | solution.py:58
  155.7 0.7 transpose_reshape_broadcast_in_dim.6
  156.4 6.5 %all-to-all-start.2 = ((f32[32,1,32]{2,1,0:T(1,128)}), f32[32,1,32]{2,1,0:T(1,128)S(1)}, u32[]{:S(2)}, u32[]{:S(2)}) async-start(f32[32,1,32]{2,1,0:T(1,128)} %transpose_reshape_broadcast_in_dim.6), calls=%async_computation.2 | async-start | bytes 32768 | tf_op jit(solution)/shard_map/all_to_all | solution.py:30
  162.9 60.7 %all-gather.5.cloned.1.call-done = bf16[2048,1024]{0,1:T(8,128)(2,1)} async-done(((bf16[2048,32]{0,1:T(8,128)(2,1)}), bf16[2048,1024]{0,1:T(8,128)(2,1)}) %all-gather.5.cloned.1.call-update) | async-done | bytes 4194320 | tf_op jit(solution)/shard_map/all_gather | solution.py:98
  223.5 3.7 %fusion.22 = f32[1024]{0:T(1024)S(1)} fusion(bf16[2048,1024]{0,1:T(8,128)(2,1)} %all-gather.5.cloned.1.call-done, bf16[128,2050]{1,0:T(8,128)(2,1)S(1)} %all_gather.9, f32[128]{0:T(128)S(1)} %get-tuple-element.7, f32[128]{0:T(128)S(1)} %get-tuple-element.6), kind=kOutput, calls=%fused_computation.40 | convolution fusion | flops 537394176 | bytes 4723712 | tf_op jit(solution)/shard_map/dot_general | solution.py:58
  227.3 0.7 transpose_reshape_broadcast_in_dim.7
  228.0 6.5 %all-to-all-start.5 = ((f32[32,1,32]{2,1,0:T(1,128)}), f32[32,1,32]{2,1,0:T(1,128)S(1)}, u32[]{:S(2)}, u32[]{:S(2)}) async-start(f32[32,1,32]{2,1,0:T(1,128)} %transpose_reshape_broadcast_in_dim.7), calls=%async_computation.5 | async-start | bytes 32768 | tf_op jit(solution)/shard_map/all_to_all | solution.py:30
  234.5 7.8 %all-to-all-done.5 = f32[32,1,32]{2,1,0:T(1,128)S(1)} async-done(((f32[32,1,32]{2,1,0:T(1,128)}), f32[32,1,32]{2,1,0:T(1,128)S(1)}, u32[]{:S(2)}, u32[]{:S(2)}) %all-to-all-start.5) | async-done | bytes 4128 | tf_op jit(solution)/shard_map/all_to_all | solution.py:30
  242.3 0.6 pad_maximum_fusion
  (42 shorter events, 2.6 us)
Async XLA Ops:
  6.5 57.7 %copy-start = (bf16[1,128,512]{2,1,0:T(8,128)(2,1)S(1)}, bf16[1,128,512]{2,1,0:T(8,128)(2,1)}, u32[]{:S(2)}) copy-start(bf16[1,128,512]{2,1,0:T(8,128)(2,1)} %param.15) | copy-start | bytes 393220
  9.1 28.7 %all-to-all-start = ((bf16[16,32,512]{2,0,1:T(8,128)(2,1)}), bf16[16,32,512]{2,0,1:T(8,128)(2,1)S(1)}, u32[]{:S(2)}, u32[]{:S(2)}) async-start(bf16[16,32,512]{2,0,1:T(8,128)(2,1)} %copy.64), calls=%async_computation | async-start | bytes 1048576 | tf_op jit(solution)/shard_map/all_to_all | solution.py:79
  22.1 21.2 %copy-start.8 = (s32[1,4]{1,0:T(1,128)S(1)}, s32[1,4]{1,0:T(1,128)}, u32[]{:S(2)}) copy-start(s32[1,4]{1,0:T(1,128)} %param.12) | copy-start | bytes 52
  22.1 21.3 %copy-start.2 = (f32[1,3,512]{2,0,1:T(1,128)S(1)}, f32[1,3,512]{2,0,1:T(1,128)}, u32[]{:S(2)}) copy-start(f32[1,3,512]{2,0,1:T(1,128)} %param.14) | copy-start | bytes 18436
  37.8 21.2 %all-to-all-start.3 = ((bf16[16,32,512]{2,0,1:T(8,128)(2,1)}), bf16[16,32,512]{2,0,1:T(8,128)(2,1)S(1)}, u32[]{:S(2)}, u32[]{:S(2)}) async-start(bf16[16,32,512]{2,0,1:T(8,128)(2,1)} %copy.72), calls=%async_computation.3 | async-start | bytes 1048576 | tf_op jit(solution)/shard_map/all_to_all | solution.py:79
  43.3 108.7 %all-gather.3.cloned.1.call-start = ((), (), s32[]{:S(2)}) async-start(), calls=%async_computation.6 | async-start | bytes 4325376 | tf_op jit(solution)/shard_map/all_gather | solution.py:98
  60.2 1.7 copy-start.6
  63.7 1.4 copy-start.7
  67.2 0.8 copy-start.5
  68.2 33.7 %copy-start.3 = (bf16[8]{0:T(256)(128)(2,1)S(1)}, bf16[8]{0:T(256)(128)(2,1)}, u32[]{:S(2)}) copy-start(bf16[8]{0:T(256)(128)(2,1)} %param.18) | copy-start | bytes 52
  68.2 33.8 %copy-start.4 = (bf16[8]{0:T(256)(128)(2,1)S(1)}, bf16[8]{0:T(256)(128)(2,1)}, u32[]{:S(2)}) copy-start(bf16[8]{0:T(256)(128)(2,1)} %param.19) | copy-start | bytes 52
  68.3 33.9 %copy-start.1 = (bf16[8,2048]{1,0:T(8,128)(2,1)S(1)}, bf16[8,2048]{1,0:T(8,128)(2,1)}, u32[]{:S(2)}) copy-start(bf16[8,2048]{1,0:T(8,128)(2,1)} %param.17) | copy-start | bytes 98308
  88.3 135.2 %all-gather.5.cloned.1.call-start = ((), (), s32[]{:S(2)}) async-start(), calls=%async_computation.7 | async-start | bytes 4325376 | tf_op jit(solution)/shard_map/all_gather | solution.py:98
  156.4 71.6 %all-to-all-start.2 = ((f32[32,1,32]{2,1,0:T(1,128)}), f32[32,1,32]{2,1,0:T(1,128)S(1)}, u32[]{:S(2)}, u32[]{:S(2)}) async-start(f32[32,1,32]{2,1,0:T(1,128)} %transpose_reshape_broadcast_in_dim.6), calls=%async_computation.2 | async-start | bytes 32768 | tf_op jit(solution)/shard_map/all_to_all | solution.py:30
  228.0 14.3 %all-to-all-start.5 = ((f32[32,1,32]{2,1,0:T(1,128)}), f32[32,1,32]{2,1,0:T(1,128)S(1)}, u32[]{:S(2)}, u32[]{:S(2)}) async-start(f32[32,1,32]{2,1,0:T(1,128)} %transpose_reshape_broadcast_in_dim.7), calls=%async_computation.5 | async-start | bytes 32768 | tf_op jit(solution)/shard_map/all_to_all | solution.py:30
Sparse Core Ops, SparseCore 0:
  88.4 63.5 all-gather.2
  154.1 69.3 all-gather.4
where the time goes:
time: 250 us
  waiting for transfers between devices  109 us (44%)
  blocking collectives  69 us (28%)
  starting transfers between devices  31.5 us (13%)
  matrix products  15.5 us (6%)
  between operations  13.7 us (5%)
  local copies, waits for them, and re-layouts  9.29 us (4%)
    all_gather x2, waiting for transfers between devices, on_device(): lax.all_gather(mixed, 'rank', axis=1, tiled=True)  72.2 us
    all_gather x1, blocking collectives, side_by_side(): whole = lax.all_gather(both, axis, axis=dim, tiled=True)  38 us
    all_to_all x2, blocking collectives, on_device(): lax.all_to_all(compressed, 'tower', split_axis=1, concat_axis=0, tiled=True)  31 us
    all_to_all x2, waiting for transfers between devices, on_device(): lax.all_to_all(pooled[batch], 'rank', split_axis=1, concat_axis=0, tiled=...  29.4 us
    all_to_all x2, starting transfers between devices, on_device(): lax.all_to_all(pooled[batch], 'rank', split_axis=1, concat_axis=0, tiled=...  18.4 us
    all_to_all x2, starting transfers between devices, summed_on_arrival(): lax.all_to_all(parts, axis, split_axis=0, concat_axis=0, tiled=True)  13 us
    all_to_all x2, waiting for transfers between devices, summed_on_arrival(): lax.all_to_all(parts, axis, split_axis=0, concat_axis=0, tiled=True)  7.8 us
    dot_general x2, matrix products, logit_terms(): jnp.dot(hidden_rows, features, preferred_element_type=jnp.float32)  7.43 us
  transfers between devices with their start and end apart: 6, of which 5 were waited for; matrix products, arithmetic and copies ran while one was open for 5% of the time, Pallas kernels for 0%

commit v1 on v0

--- a/solution.py
+++ b/solution.py
@@ -95,7 +95,12 @@
         tower_parts = lax.all_to_all(compressed, "tower", split_axis=1, concat_axis=0, tiled=True)
         mixed = interact(tower_parts)
         partial_value = logit_terms(
-            hidden_rows, hidden_bias, hidden_out, lax.all_gather(mixed, "rank", axis=1, tiled=True)
+            hidden_rows,
+            hidden_bias,
+            hidden_out,
+            jnp.concatenate(
+                lax.all_to_all(jnp.stack([mixed] * lax.axis_size("rank")), "rank", 0, 0), axis=1
+            ),
         )
         logit_row = summed_on_arrival(partial_value, "rank", 1)
         results.append(logit_row)

time: 250 us -> 364 us (1.46)
  blocking collectives: 69 us -> 127 us
  waiting for transfers between devices: 109 us -> 152 us
  starting transfers between devices: 31.5 us -> 53.3 us
  between operations: 13.7 us -> 0.31 us
  local copies, waits for them, and re-layouts: 9.29 us -> 13 us
    all_to_all x0 -> x3, waiting for transfers between devices: none -> 111 us  [the longest x2 102 us: on_device(): lax.all_to_all(jnp.stack([mixed] * lax.axis_size('rank')), 'rank', 0, 0)]
    all_gather x2 -> x0, waiting for transfers between devices: 72.2 us -> none  [on_device(): lax.all_gather(mixed, 'rank', axis=1, tiled=True)]
    all_gather x1, blocking collectives: 38 us -> 108 us  [side_by_side(): whole = lax.all_gather(both, axis, axis=dim, tiled=True)]
    all_to_all x0 -> x3, starting transfers between devices: none -> 16.5 us  [the longest x2 13 us: on_device(): lax.all_to_all(jnp.stack([mixed] * lax.axis_size('rank')), 'rank', 0, 0)]
    all_to_all x2 -> x1, blocking collectives: 31 us -> 18.6 us  [on_device(): lax.all_to_all(compressed, 'tower', split_axis=1, concat_axis=0, tiled=True)]
    all_to_all x2, starting transfers between devices: 13 us -> 18.3 us  [summed_on_arrival(): lax.all_to_all(parts, axis, split_axis=0, concat_axis=0, tiled=True)]
    another operation x0 -> x2, local copies, waits for them, and re-layouts: none -> 5 us  [on_device(): jnp.stack([mixed] * lax.axis_size('rank'))]
  transfers between devices with their start and end apart: 6 -> 7, of which waited for: 5 -> 6; matrix products, arithmetic and copies ran while one was open for 5% -> 3% of each run, Pallas kernels for 0% -> 0%
where the time goes in v1:
time: 364 us; the launch traced here: 363 us
  waiting for transfers between devices  152 us (42%)
  blocking collectives  127 us (35%)
  starting transfers between devices  53.3 us (15%)
  matrix products  15.6 us (4%)
  local copies, waits for them, and re-layouts  13 us (4%)
    all_gather x1, blocking collectives, side_by_side(): whole = lax.all_gather(both, axis, axis=dim, tiled=True)  108 us
    all_to_all x2, waiting for transfers between devices, on_device(): lax.all_to_all(jnp.stack([mixed] * lax.axis_size('rank')), 'rank', 0, 0)  102 us
    all_to_all x2, waiting for transfers between devices, on_device(): lax.all_to_all(pooled[batch], 'rank', split_axis=1, concat_axis=0, tiled=...  29.5 us
    all_to_all x1, blocking collectives, on_device(): lax.all_to_all(compressed, 'tower', split_axis=1, concat_axis=0, tiled=True)  18.6 us
    all_to_all x2, starting transfers between devices, on_device(): lax.all_to_all(pooled[batch], 'rank', split_axis=1, concat_axis=0, tiled=...  18.4 us
    all_to_all x2, starting transfers between devices, summed_on_arrival(): lax.all_to_all(parts, axis, split_axis=0, concat_axis=0, tiled=True)  18.3 us
    all_to_all x2, starting transfers between devices, on_device(): lax.all_to_all(jnp.stack([mixed] * lax.axis_size('rank')), 'rank', 0, 0)  13 us
    all_to_all x2, waiting for transfers between devices, summed_on_arrival(): lax.all_to_all(parts, axis, split_axis=0, concat_axis=0, tiled=True)  11.2 us
  transfers between devices with their start and end apart: 7, of which 6 were waited for; matrix products, arithmetic and copies ran while one was open for 3% of the time, Pallas kernels for 0%

profile of v1, /device:TPU:1, one launch (start us, length us, event | category | flops | bytes accessed | tf_op | source)
XLA Modules:
  0.0 363.1 jit_solution(4905447913745403523)
XLA Ops:
  0.0 1.3 fusion.58
  1.5 1.1 copy.66
  2.6 13.0 %all-to-all-start = ((bf16[16,32,512]{2,0,1:T(8,128)(2,1)}), bf16[16,32,512]{2,0,1:T(8,128)(2,1)S(1)}, u32[]{:S(2)}, u32[]{:S(2)}) async-start(bf16[16,32,512]{2,0,1:T(8,128)(2,1)} %copy.66), calls=%async_computation | async-start | bytes 1048576 | tf_op jit(solution)/shard_map/all_to_all | solution.py:79
  15.7 1.1 copy.74
  16.8 14.4 %all-to-all-done = bf16[16,32,512]{2,0,1:T(8,128)(2,1)S(1)} async-done(((bf16[16,32,512]{2,0,1:T(8,128)(2,1)}), bf16[16,32,512]{2,0,1:T(8,128)(2,1)S(1)}, u32[]{:S(2)}, u32[]{:S(2)}) %all-to-all-start) | async-done | bytes 524320 | tf_op jit(solution)/shard_map/all_to_all | solution.py:79
  31.3 5.5 %all-to-all-start.4 = ((bf16[16,32,512]{2,0,1:T(8,128)(2,1)}), bf16[16,32,512]{2,0,1:T(8,128)(2,1)S(1)}, u32[]{:S(2)}, u32[]{:S(2)}) async-start(bf16[16,32,512]{2,0,1:T(8,128)(2,1)} %copy.74), calls=%async_computation.4 | async-start | bytes 1048576 | tf_op jit(solution)/shard_map/all_to_all | solution.py:79
  36.8 0.6 gather_fusion
  37.4 15.1 %all-to-all-done.4 = bf16[16,32,512]{2,0,1:T(8,128)(2,1)S(1)} async-done(((bf16[16,32,512]{2,0,1:T(8,128)(2,1)}), bf16[16,32,512]{2,0,1:T(8,128)(2,1)S(1)}, u32[]{:S(2)}, u32[]{:S(2)}) %all-to-all-start.4) | async-done | bytes 524320 | tf_op jit(solution)/shard_map/all_to_all | solution.py:79
  52.4 0.6 gather_fusion.1
  53.6 1.7 fusion.11
  55.9 1.3 fusion.14
  57.7 0.9 copy-done.7
  58.6 2.0 multiply_reduce_fusion
  60.7 0.8 multiply_reduce_fusion.1
  61.5 0.8 multiply_convert_fusion.1
  62.3 18.6 %all_to_all.78 = bf16[128,16,32]{0,2,1:T(8,128)(2,1)S(1)} all-to-all(bf16[128,16,32]{0,2,1:T(8,128)(2,1)S(1)} %bitcast.180), channel_id=1, replica_groups=mesh['tower'=16,'rank'=32] {'tower'}, dimensions={1} | all-to-all | bytes 262144 | tf_op jit(solution)/shard_map/all_to_all | solution.py:95
  81.0 3.5 all-to-all-start.5
  85.1 9.0 %all-to-all-done.5 = bf16[128,16,32]{0,2,1:T(8,128)(2,1)S(1)} async-done(((bf16[128,16,32]{0,2,1:T(8,128)(2,1)}), bf16[128,16,32]{0,2,1:T(8,128)(2,1)S(1)}, u32[]{:S(2)}, u32[]{:S(2)}) %all-to-all-start.5) | async-done | bytes 131104 | tf_op jit(solution)/shard_map/all_to_all | solution.py:95
  94.1 2.5 stack.10
  96.7 7.4 %all-to-all-start.2 = ((bf16[32,2048,32]{1,2,0:T(8,128)(2,1)}), bf16[32,2048,32]{1,2,0:T(8,128)(2,1)}, u32[]{:S(2)}, u32[]{:S(2)}) async-start(bf16[32,2048,32]{1,2,0:T(8,128)(2,1)} %stack.10), calls=%async_computation.2 | async-start | bytes 8388608 | tf_op jit(solution)/shard_map/all_to_all | solution.py:102
  104.7 102.4 %all-to-all-done.2 = bf16[32,2048,32]{1,2,0:T(8,128)(2,1)} async-done(((bf16[32,2048,32]{1,2,0:T(8,128)(2,1)}), bf16[32,2048,32]{1,2,0:T(8,128)(2,1)}, u32[]{:S(2)}, u32[]{:S(2)}) %all-to-all-start.2) | async-done | bytes 4194336 | tf_op jit(solution)/shard_map/all_to_all | solution.py:102
  207.1 2.5 stack.12
  209.6 5.6 %all-to-all-start.6 = ((bf16[32,2048,32]{1,2,0:T(8,128)(2,1)}), bf16[32,2048,32]{1,2,0:T(8,128)(2,1)}, u32[]{:S(2)}, u32[]{:S(2)}) async-start(bf16[32,2048,32]{1,2,0:T(8,128)(2,1)} %stack.12), calls=%async_computation.6 | async-start | bytes 8388608 | tf_op jit(solution)/shard_map/all_to_all | solution.py:102
  215.6 108.5 %all_gather.3 = bf16[128,2050]{1,0:T(8,128)(2,1)S(1)} all-gather(bf16[8,2050]{1,0:T(8,128)(2,1)S(1)} %concatenate.3), channel_id=1, replica_groups=mesh['tower'=16,'rank'=32] {'tower'}, dimensions={0}, use_global_device_ids=true | all-gather | bytes 557600 | tf_op jit(solution)/shard_map/all_gather | solution.py:17
  324.2 3.7 %fusion.23 = f32[1024]{0:T(1024)S(1)} fusion(bf16[2048,1024]{0,1:T(8,128)(2,1)} %bitcast.23, bf16[128,2050]{1,0:T(8,128)(2,1)S(1)} %all_gather.3, f32[128]{0:T(128)S(1)} %get-tuple-element.7, f32[128]{0:T(128)S(1)} %get-tuple-element.6), kind=kOutput, calls=%fused_computation.41 | convolution fusion | flops 537394176 | bytes 4723712 | tf_op jit(solution)/shard_map/dot_general | solution.py:58
  327.9 0.7 transpose_reshape_broadcast_in_dim.6
  328.6 13.4 %all-to-all-start.3 = ((f32[32,1,32]{2,1,0:T(1,128)}), f32[32,1,32]{2,1,0:T(1,128)S(1)}, u32[]{:S(2)}, u32[]{:S(2)}) async-start(f32[32,1,32]{2,1,0:T(1,128)} %transpose_reshape_broadcast_in_dim.6), calls=%async_computation.3 | async-start | bytes 32768 | tf_op jit(solution)/shard_map/all_to_all | solution.py:30
  342.0 3.7 %fusion.22 = f32[1024]{0:T(1024)S(1)} fusion(bf16[2048,1024]{0,1:T(8,128)(2,1)} %bitcast.38, bf16[128,2050]{1,0:T(8,128)(2,1)S(1)} %all_gather.3, f32[128]{0:T(128)S(1)} %get-tuple-element.7, f32[128]{0:T(128)S(1)} %get-tuple-element.6), kind=kOutput, calls=%fused_computation.40 | convolution fusion | flops 537394176 | bytes 4723712 | tf_op jit(solution)/shard_map/dot_general | solution.py:58
  345.7 0.7 transpose_reshape_broadcast_in_dim.7
  346.4 3.4 all-to-all-done.3
  349.8 4.9 %all-to-all-start.7 = ((f32[32,1,32]{2,1,0:T(1,128)}), f32[32,1,32]{2,1,0:T(1,128)S(1)}, u32[]{:S(2)}, u32[]{:S(2)}) async-start(f32[32,1,32]{2,1,0:T(1,128)} %transpose_reshape_broadcast_in_dim.7), calls=%async_computation.7 | async-start | bytes 32768 | tf_op jit(solution)/shard_map/all_to_all | solution.py:30
  354.8 7.8 %all-to-all-done.7 = f32[32,1,32]{2,1,0:T(1,128)S(1)} async-done(((f32[32,1,32]{2,1,0:T(1,128)}), f32[32,1,32]{2,1,0:T(1,128)S(1)}, u32[]{:S(2)}, u32[]{:S(2)}) %all-to-all-start.7) | async-done | bytes 4128 | tf_op jit(solution)/shard_map/all_to_all | solution.py:30
  (43 shorter events, 4.4 us)
Async XLA Ops:
  0.0 57.7 %copy-start = (bf16[1,128,512]{2,1,0:T(8,128)(2,1)S(1)}, bf16[1,128,512]{2,1,0:T(8,128)(2,1)}, u32[]{:S(2)}) copy-start(bf16[1,128,512]{2,1,0:T(8,128)(2,1)} %param.15) | copy-start | bytes 393220
  2.6 28.7 %all-to-all-start = ((bf16[16,32,512]{2,0,1:T(8,128)(2,1)}), bf16[16,32,512]{2,0,1:T(8,128)(2,1)S(1)}, u32[]{:S(2)}, u32[]{:S(2)}) async-start(bf16[16,32,512]{2,0,1:T(8,128)(2,1)} %copy.66), calls=%async_computation | async-start | bytes 1048576 | tf_op jit(solution)/shard_map/all_to_all | solution.py:79
  15.6 21.2 %copy-start.8 = (s32[1,4]{1,0:T(1,128)S(1)}, s32[1,4]{1,0:T(1,128)}, u32[]{:S(2)}) copy-start(s32[1,4]{1,0:T(1,128)} %param.12) | copy-start | bytes 52
  15.6 21.2 %copy-start.2 = (f32[1,3,512]{2,0,1:T(1,128)S(1)}, f32[1,3,512]{2,0,1:T(1,128)}, u32[]{:S(2)}) copy-start(f32[1,3,512]{2,0,1:T(1,128)} %param.14) | copy-start | bytes 18436
  31.3 21.2 %all-to-all-start.4 = ((bf16[16,32,512]{2,0,1:T(8,128)(2,1)}), bf16[16,32,512]{2,0,1:T(8,128)(2,1)S(1)}, u32[]{:S(2)}, u32[]{:S(2)}) async-start(bf16[16,32,512]{2,0,1:T(8,128)(2,1)} %copy.74), calls=%async_computation.4 | async-start | bytes 1048576 | tf_op jit(solution)/shard_map/all_to_all | solution.py:79
  53.6 1.7 copy-start.6
  57.2 1.4 copy-start.7
  60.6 0.8 copy-start.5
  81.0 13.2 %all-to-all-start.5 = ((bf16[128,16,32]{0,2,1:T(8,128)(2,1)}), bf16[128,16,32]{0,2,1:T(8,128)(2,1)S(1)}, u32[]{:S(2)}, u32[]{:S(2)}) async-start(bf16[128,16,32]{0,2,1:T(8,128)(2,1)} %bitcast.33), calls=%async_computation.5 | async-start | bytes 262144 | tf_op jit(solution)/shard_map/all_to_all | solution.py:95
  96.7 110.5 %all-to-all-start.2 = ((bf16[32,2048,32]{1,2,0:T(8,128)(2,1)}), bf16[32,2048,32]{1,2,0:T(8,128)(2,1)}, u32[]{:S(2)}, u32[]{:S(2)}) async-start(bf16[32,2048,32]{1,2,0:T(8,128)(2,1)} %stack.10), calls=%async_computation.2 | async-start | bytes 8388608 | tf_op jit(solution)/shard_map/all_to_all | solution.py:102
  209.6 5.6 %copy-start.3 = (bf16[8]{0:T(256)(128)(2,1)S(1)}, bf16[8]{0:T(256)(128)(2,1)}, u32[]{:S(2)}) copy-start(bf16[8]{0:T(256)(128)(2,1)} %param.18) | copy-start | bytes 52
  209.6 5.7 %copy-start.4 = (bf16[8]{0:T(256)(128)(2,1)S(1)}, bf16[8]{0:T(256)(128)(2,1)}, u32[]{:S(2)}) copy-start(bf16[8]{0:T(256)(128)(2,1)} %param.19) | copy-start | bytes 52
  209.6 5.8 %copy-start.1 = (bf16[8,2048]{1,0:T(8,128)(2,1)S(1)}, bf16[8,2048]{1,0:T(8,128)(2,1)}, u32[]{:S(2)}) copy-start(bf16[8,2048]{1,0:T(8,128)(2,1)} %param.17) | copy-start | bytes 98308
  209.6 119.0 %all-to-all-start.6 = ((bf16[32,2048,32]{1,2,0:T(8,128)(2,1)}), bf16[32,2048,32]{1,2,0:T(8,128)(2,1)}, u32[]{:S(2)}, u32[]{:S(2)}) async-start(bf16[32,2048,32]{1,2,0:T(8,128)(2,1)} %stack.12), calls=%async_computation.6 | async-start | bytes 8388608 | tf_op jit(solution)/shard_map/all_to_all | solution.py:102
  328.6 21.2 %all-to-all-start.3 = ((f32[32,1,32]{2,1,0:T(1,128)}), f32[32,1,32]{2,1,0:T(1,128)S(1)}, u32[]{:S(2)}, u32[]{:S(2)}) async-start(f32[32,1,32]{2,1,0:T(1,128)} %transpose_reshape_broadcast_in_dim.6), calls=%async_computation.3 | async-start | bytes 32768 | tf_op jit(solution)/shard_map/all_to_all | solution.py:30
  349.8 12.7 %all-to-all-start.7 = ((f32[32,1,32]{2,1,0:T(1,128)}), f32[32,1,32]{2,1,0:T(1,128)S(1)}, u32[]{:S(2)}, u32[]{:S(2)}) async-start(f32[32,1,32]{2,1,0:T(1,128)} %transpose_reshape_broadcast_in_dim.7), calls=%async_computation.7 | async-start | bytes 32768 | tf_op jit(solution)/shard_map/all_to_all | solution.py:30
